TPU v7x, 32 devices: a whole 2x2x4 slice. The times are simulated.
32 devices in a mesh: dp: 8 (over z, x), mp: 4 (over y, core).
Axes of the slice: x: 2, y: 2, z: 4, core: 2. Of those that a mesh axis runs over, the one named last changes fastest.
Arguments:
- block_input: bfloat16 [8, 8192, 512], P('dp', 'mp'), may hold values from -6 to 6
- routes: int32 [8, 8192, 2], P('dp', 'mp'), may hold values from 0 to 7, all different within a row; in each aligned block of 2048 rows (0 to 2047, 2048 to 4095, ..., all dimensions but the last counted through in order) at most 1024 rows name the same one
- lengths: int32 [8], P('dp'), may hold values from 6145 to 8192, as said below
- first_gain: float32 [512], replicated, may hold values from 0.25 to 1.75
- first_bias: float32 [512], replicated, may hold values from -1.5 to 1.5
- router_weight: bfloat16 [512, 8], replicated, may hold values from -0.1875 to 0.1875
- shared_proj: bfloat16 [512, 128], replicated, may hold values from -0.25 to 0.25
- query_weight: bfloat16 [64, 4096], P('mp', 'dp'), may hold values from -0.25 to 0.25
- output_weight: bfloat16 [64, 4096], P('mp', 'dp'), may hold values from -40 to 40
- second_gain: float32 [512], replicated, may hold values from 0.25 to 1.75
- second_bias: float32 [512], replicated, may hold values from -1.5 to 1.5
- expand_weight: bfloat16 [512, 2048], P(None, 'mp'), may hold values from -0.25 to 0.25
- expand_bias: bfloat16 [2048], P('mp'), may hold values from -1.5 to 1.5
- reduce_weight: bfloat16 [2048, 512], P('mp'), may hold values from -0.125 to 0.125
- reduce_bias: bfloat16 [512], replicated, may hold values from -1.5 to 1.5
- upstream_grad: bfloat16 [8, 8192, 512], P('dp', 'mp'), may hold values from -6 to 6
Outputs:
- block_output: bfloat16 [8, 8192, 512], P('dp', 'mp')
- input_grad: float32 [8, 8192, 512], P('dp', 'mp')
- first_gain_grad: float32 [512], P('mp')
- first_bias_grad: float32 [512], P('mp')
- router_grad: float32 [512, 8], P('mp')
- shared_grad: float32 [512, 128], P('mp')
- query_weight_grad: float32 [64, 4096], P('mp', 'dp')
- output_weight_grad: float32 [64, 4096], P('mp', 'dp')
- second_gain_grad: float32 [512], P('mp')
- second_bias_grad: float32 [512], P('mp')
- expand_weight_grad: float32 [512, 2048], P(None, 'mp')
- expand_bias_grad: float32 [2048], P('mp')
- reduce_weight_grad: float32 [2048, 512], P('mp')
- reduce_bias_grad: float32 [512], P('mp')
Inputs may be any that keep to these rules, and one draw needn't show every extreme that they name: `routes`: the two experts of a position differ. In each aligned block of 2048 positions of a sequence, no expert is named by more than 1024 positions, a bound that some block reaches. `lengths`: one sequence has length 8192 and another 3 * 2048 + 1.
All inputs are finite; a program needn't handle non-finite values.
Results may differ from a plain program's by a relative error of at most 0.013.
Values may be sent and summed in bfloat16 or wider, within the bound.
No kernel may reach another device: no remote copies, remote signals or barrier semaphores. Data moves between devices by JAX's collectives and lax.ppermute only.
A program may use at most 256 MiB of HBM per device.

v0:
```python
import jax
import jax.numpy as jnp
from jax import lax
from jax.sharding import PartitionSpec as P

norm_epsilon = 1e-05
score_scale = 0.125
masked_score = -1e30
highest = lax.Precision.HIGHEST


def in_blocks(value, dim, devices):
    before, after = (value.shape[:dim], value.shape[dim + 1 :])
    return jnp.moveaxis(value.reshape(*before, devices, -1, *after), dim, 0)


def sent_and_summed(value, axis, dim):
    parts = in_blocks(value, dim, lax.axis_size(axis))
    arrived = lax.all_to_all(parts, axis, split_axis=0, concat_axis=0, tiled=True)
    return arrived.astype(jnp.float32).sum(axis=0)


def side_by_side(arrays, axis, dim, along):
    both = jnp.concatenate(arrays, axis=along)
    whole, at, done = (sent_and_summed(both, axis, dim), 0, [])
    for a in arrays:
        done.append(lax.slice_in_dim(whole, at, at + a.shape[along], axis=along))
        at += a.shape[along]
    return tuple(done)


def layer_norm(values, gain, bias):
    centred = values - jnp.mean(values, axis=-1, keepdims=True)
    inverse = lax.rsqrt(jnp.mean(centred * centred, axis=-1, keepdims=True) + norm_epsilon)
    normal = centred * inverse
    return (normal * gain + bias, normal, inverse)


def norm_back(grad, normal, inverse, gain):
    scaled = grad * gain
    back = inverse * (
        scaled
        - jnp.mean(scaled, axis=-1, keepdims=True)
        - normal * jnp.mean(scaled * normal, axis=-1, keepdims=True)
    )
    return (back, jnp.sum(grad * normal, axis=0), jnp.sum(grad, axis=0))


def gelu_tanh(values):
    return jax.nn.gelu(values, approximate=True)


def on_device(
    block_input,
    routes,
    lengths,
    first_gain,
    first_bias,
    router_weight,
    shared_proj,
    query_weight,
    output_weight,
    second_gain,
    second_bias,
    expand_weight,
    expand_bias,
    reduce_weight,
    reduce_bias,
    upstream_grad,
):
    own_tokens = block_input.shape[1]
    width = block_input.shape[2]
    experts = router_weight.shape[1]
    head_width = query_weight.shape[0] * lax.axis_size("mp")
    capacity = own_tokens // 2
    route_rows = 2 * own_tokens
    source = block_input.reshape(own_tokens, width).astype(jnp.float32)
    first_out, first_normal, first_scale = layer_norm(source, first_gain, first_bias)
    normed = first_out.astype(jnp.bfloat16)
    logits = jnp.dot(normed, router_weight, preferred_element_type=jnp.float32)
    own_pairs = jnp.dot(normed, shared_proj, preferred_element_type=jnp.float32).astype(
        jnp.bfloat16
    )
    key_pairs, query_rows, output_rows, expand_full, expand_bias_full, reduce_full = (
        lax.all_gather(own_pairs, "mp", axis=0, tiled=True),
        lax.all_gather(query_weight, "mp", axis=0, tiled=True),
        lax.all_gather(output_weight, "mp", axis=0, tiled=True),
        lax.all_gather(expand_weight, "mp", axis=1, tiled=True),
        lax.all_gather(expand_bias, "mp", axis=0, tiled=True),
        lax.all_gather(reduce_weight, "mp", axis=0, tiled=True),
    )
    route_flat = routes.reshape(route_rows)
    route_hot = (route_flat[:, None] == jnp.arange(experts, dtype=jnp.int32)[None, :]).astype(
        jnp.int32
    )
    earlier = jnp.cumsum(route_hot, axis=0) - route_hot
    position = jnp.sum(earlier * route_hot, axis=1)
    target = route_flat * capacity + position
    slot_source = (
        jnp.zeros((experts * capacity,), jnp.int32)
        .at[target]
        .set(jnp.arange(route_rows, dtype=jnp.int32))
    )
    slot_live = jnp.zeros((experts * capacity,), jnp.bfloat16).at[target].set(1.0)
    slot_token = slot_source // 2
    slot_rows = normed[slot_token] * slot_live[:, None]
    hot_float = route_hot.reshape(own_tokens, 2, experts).astype(jnp.float32)
    chosen = jnp.einsum("tse,te->ts", hot_float, logits, precision=highest)
    gates = jax.nn.softmax(chosen, axis=1)
    query_all, output_all = (
        lax.all_gather(query_rows, "dp", axis=1, tiled=True),
        lax.all_gather(output_rows, "dp", axis=1, tiled=True),
    )
    query_slots = jnp.einsum(
        "ecd,hed->ech",
        slot_rows.reshape(experts, capacity, width),
        query_all.reshape(head_width, experts, width),
        preferred_element_type=jnp.float32,
    ).reshape(experts * capacity, head_width)
    query_round = query_slots.astype(jnp.bfloat16)
    queries = query_round[target]
    keys = key_pairs[:, :head_width]
    value_rows = key_pairs[:, head_width:]
    key_count = key_pairs.shape[0]
    key_live = jnp.arange(key_count, dtype=jnp.int32) < lengths[0]
    block = min(512, route_rows)
    blocks = route_rows // block
    query_blocks = queries.reshape(blocks, block, head_width)

    def scores_of(query_block):
        raw = (
            jnp.einsum("qh,kh->qk", query_block, keys, preferred_element_type=jnp.float32)
            * score_scale
        )
        return jnp.where(key_live[None, :], raw, masked_score)

    def attend(query_block):
        scores = scores_of(query_block)
        peak = jnp.max(scores, axis=1, keepdims=True)
        weights = jnp.exp(scores - peak)
        total = jnp.sum(weights, axis=1, keepdims=True)
        attention = (weights / total).astype(jnp.bfloat16)
        mixed_block = jnp.dot(attention, value_rows, preferred_element_type=jnp.float32).astype(
            jnp.bfloat16
        )
        return (mixed_block, (peak + jnp.log(total))[:, 0])

    mixed_blocks, log_totals = lax.map(attend, query_blocks)
    mixed = mixed_blocks.reshape(route_rows, head_width)
    mix_slots = mixed[slot_source] * slot_live[:, None]
    branch_slots = (
        jnp.einsum(
            "ech,hed->ecd",
            mix_slots.reshape(experts, capacity, head_width),
            output_all.reshape(head_width, experts, width),
            preferred_element_type=jnp.float32,
        )
        .astype(jnp.bfloat16)
        .reshape(experts * capacity, width)
    )
    branch = branch_slots[target].reshape(own_tokens, 2, width).astype(jnp.float32)
    attended = jnp.einsum("ts,tsd->td", gates, branch, precision=highest)
    middle = source + attended
    second_out, second_normal, second_scale = layer_norm(middle, second_gain, second_bias)
    normed_two = second_out.astype(jnp.bfloat16)
    expanded = jnp.dot(
        normed_two, expand_full, preferred_element_type=jnp.float32
    ) + expand_bias_full.astype(jnp.float32)
    active, slope_pull = jax.vjp(gelu_tanh, expanded)
    rounded_active = active.astype(jnp.bfloat16)
    reduced = jnp.dot(
        rounded_active, reduce_full, preferred_element_type=jnp.float32
    ) + reduce_bias.astype(jnp.float32)
    block_output = (middle + reduced).astype(jnp.bfloat16).reshape(1, own_tokens, width)
    upstream = upstream_grad.reshape(own_tokens, width)
    reduce_grad = jnp.einsum(
        "tf,td->fd", rounded_active, upstream, preferred_element_type=jnp.float32
    )
    reduce_bias_grad = jnp.sum(upstream.astype(jnp.float32), axis=0)
    active_grad = jnp.einsum("td,fd->tf", upstream, reduce_full, preferred_element_type=jnp.float32)
    expanded_grad = slope_pull(active_grad)[0].astype(jnp.bfloat16)
    expand_grad = jnp.einsum(
        "td,tf->df", normed_two, expanded_grad, preferred_element_type=jnp.float32
    )
    expand_bias_grad = jnp.sum(expanded_grad.astype(jnp.float32), axis=0)
    normed_two_grad = jnp.einsum(
        "tf,df->td", expanded_grad, expand_full, preferred_element_type=jnp.float32
    )
    second_back, second_gain_grad, second_bias_grad = norm_back(
        normed_two_grad, second_normal, second_scale, second_gain
    )
    middle_grad = upstream.astype(jnp.float32) + second_back
    gate_grad = jnp.einsum("td,tsd->ts", middle_grad, branch, precision=highest)
    chosen_grad = gates * (gate_grad - jnp.sum(gates * gate_grad, axis=1, keepdims=True))
    logit_grad = jnp.einsum("ts,tse->te", chosen_grad, hot_float, precision=highest)
    router_grad = jnp.einsum("td,te->de", normed.astype(jnp.float32), logit_grad, precision=highest)
    router_back = jnp.einsum(
        "te,de->td", logit_grad, router_weight.astype(jnp.float32), precision=highest
    )
    branch_grad = (
        (gates[:, :, None] * middle_grad[:, None, :])
        .astype(jnp.bfloat16)
        .reshape(route_rows, width)
    )
    branch_grad_slots = branch_grad[slot_source] * slot_live[:, None]
    output_all_grad = jnp.einsum(
        "ech,ecd->hed",
        mix_slots.reshape(experts, capacity, head_width),
        branch_grad_slots.reshape(experts, capacity, width),
        preferred_element_type=jnp.float32,
    ).reshape(head_width, experts * width)
    mix_grad_slots = jnp.einsum(
        "ecd,hed->ech",
        branch_grad_slots.reshape(experts, capacity, width),
        output_all.reshape(head_width, experts, width),
        preferred_element_type=jnp.float32,
    ).reshape(experts * capacity, head_width)
    mix_grad = mix_grad_slots.astype(jnp.bfloat16)[target]

    def attend_back(carry, block_args):
        query_block, grad_block, log_total = block_args
        attention = jnp.exp(scores_of(query_block) - log_total[:, None])
        attention_grad = jnp.einsum(
            "qh,kh->qk", grad_block, value_rows, preferred_element_type=jnp.float32
        )
        delta = jnp.sum(attention * attention_grad, axis=1, keepdims=True)
        scores_grad = (attention * (attention_grad - delta)).astype(jnp.bfloat16)
        query_grad = jnp.dot(scores_grad, keys, preferred_element_type=jnp.float32) * score_scale
        keys_grad = (
            jnp.einsum("qk,qh->kh", scores_grad, query_block, preferred_element_type=jnp.float32)
            * score_scale
        )
        values_grad = jnp.einsum(
            "qk,qh->kh",
            attention.astype(jnp.bfloat16),
            grad_block,
            preferred_element_type=jnp.float32,
        )
        return (carry + jnp.concatenate([keys_grad, values_grad], axis=1), query_grad)

    pair_grad, query_grads = lax.scan(
        attend_back,
        jnp.zeros((key_count, 2 * head_width), jnp.float32),
        (query_blocks, mix_grad.reshape(blocks, block, head_width), log_totals),
    )
    shared_pair_grad = lax.psum_scatter(
        pair_grad.astype(jnp.bfloat16), "mp", scatter_dimension=0, tiled=True
    )
    shared_grad = jnp.einsum(
        "td,tc->dc", normed, shared_pair_grad, preferred_element_type=jnp.float32
    )
    shared_back = jnp.einsum(
        "tc,dc->td", shared_pair_grad, shared_proj, preferred_element_type=jnp.float32
    )
    query_grad_round = query_grads.reshape(route_rows, head_width).astype(jnp.bfloat16)
    query_grad_slots = query_grad_round[slot_source] * slot_live[:, None]
    query_all_grad = jnp.einsum(
        "ecd,ech->hed",
        slot_rows.reshape(experts, capacity, width),
        query_grad_slots.reshape(experts, capacity, head_width),
        preferred_element_type=jnp.float32,
    ).reshape(head_width, experts * width)
    row_grad_slots = (
        jnp.einsum(
            "ech,hed->ecd",
            query_grad_slots.reshape(experts, capacity, head_width),
            query_all.reshape(head_width, experts, width),
            preferred_element_type=jnp.float32,
        )
        .astype(jnp.bfloat16)
        .reshape(experts * capacity, width)
    )
    query_term, output_term = side_by_side(
        (query_all_grad.astype(jnp.bfloat16), output_all_grad.astype(jnp.bfloat16)), "dp", 1, 0
    )
    row_grad = row_grad_slots[target].reshape(own_tokens, 2, width).astype(jnp.float32)
    normed_grad = jnp.sum(row_grad, axis=1) + shared_back + router_back
    first_back, first_gain_grad, first_bias_grad = norm_back(
        normed_grad, first_normal, first_scale, first_gain
    )
    input_grad = (middle_grad + first_back).reshape(1, own_tokens, width)
    shares = (
        lax.psum_scatter(
            query_term.astype(jnp.bfloat16), "mp", scatter_dimension=0, tiled=True
        ).astype(jnp.float32),
        lax.psum_scatter(
            output_term.astype(jnp.bfloat16), "mp", scatter_dimension=0, tiled=True
        ).astype(jnp.float32),
        lax.psum_scatter(
            expand_grad.astype(jnp.bfloat16), "mp", scatter_dimension=1, tiled=True
        ).astype(jnp.float32),
        lax.psum_scatter(
            expand_bias_grad.astype(jnp.bfloat16), "mp", scatter_dimension=0, tiled=True
        ).astype(jnp.float32),
        lax.psum_scatter(
            reduce_grad.astype(jnp.bfloat16), "mp", scatter_dimension=0, tiled=True
        ).astype(jnp.float32),
        lax.psum_scatter(
            reduce_bias_grad.astype(jnp.bfloat16), "mp", scatter_dimension=0, tiled=True
        ).astype(jnp.float32),
        lax.psum_scatter(
            shared_grad.astype(jnp.bfloat16), "mp", scatter_dimension=0, tiled=True
        ).astype(jnp.float32),
        lax.psum_scatter(
            router_grad.astype(jnp.bfloat16), "mp", scatter_dimension=0, tiled=True
        ).astype(jnp.float32),
        lax.psum_scatter(
            first_gain_grad.astype(jnp.bfloat16), "mp", scatter_dimension=0, tiled=True
        ).astype(jnp.float32),
        lax.psum_scatter(
            first_bias_grad.astype(jnp.bfloat16), "mp", scatter_dimension=0, tiled=True
        ).astype(jnp.float32),
        lax.psum_scatter(
            second_gain_grad.astype(jnp.bfloat16), "mp", scatter_dimension=0, tiled=True
        ).astype(jnp.float32),
        lax.psum_scatter(
            second_bias_grad.astype(jnp.bfloat16), "mp", scatter_dimension=0, tiled=True
        ).astype(jnp.float32),
    )
    totals = lax.psum(
        (
            shares[2],
            shares[3],
            shares[4],
            shares[5],
            shares[6],
            shares[7],
            shares[8],
            shares[9],
            shares[10],
            shares[11],
        ),
        "dp",
    )
    return (
        block_output,
        input_grad,
        totals[6],
        totals[7],
        totals[5],
        totals[4],
        shares[0],
        shares[1],
        totals[8],
        totals[9],
        totals[0],
        totals[1],
        totals[2],
        totals[3],
    )


def solution(mesh):
    placed = (
        P("dp", "mp", None),
        P("dp", "mp", None),
        P("dp"),
        P(),
        P(),
        P(),
        P(),
        P("mp", "dp"),
        P("mp", "dp"),
        P(),
        P(),
        P(None, "mp"),
        P("mp"),
        P("mp", None),
        P(),
        P("dp", "mp", None),
    )
    return jax.shard_map(
        on_device,
        mesh=mesh,
        in_specs=placed,
        out_specs=(
            P("dp", "mp", None),
            P("dp", "mp", None),
            P("mp"),
            P("mp"),
            P("mp", None),
            P("mp", None),
            P("mp", "dp"),
            P("mp", "dp"),
            P("mp"),
            P("mp"),
            P(None, "mp"),
            P("mp"),
            P("mp", None),
            P("mp"),
        ),
        check_vma=False,
    )
```

profile of v0, /device:TPU:0, one launch (start us, length us, event | category | flops | bytes accessed | tf_op | source)
XLA Modules:
  0.0 1454.3 jit_solution(10817513206052245559)
XLA Ops:
  35.5 33.7 %all_gather.28 = bf16[64,4096]{1,0:T(8,128)(2,1)} all-gather(bf16[64,512]{1,0:T(8,128)(2,1)S(1)} %all_gather.27), channel_id=1, replica_groups=mesh['dp'=8,'mp'=4] {'dp'}, dimensions={1}, use_global_device_ids=true | all-gather | bytes 589824 | tf_op jit(solution)/shard_map/all_gather | solution.py:112
  69.2 33.4 %all_gather.25 = bf16[64,4096]{1,0:T(8,128)(2,1)} all-gather(bf16[64,512]{1,0:T(8,128)(2,1)S(1)} %all_gather.24), channel_id=1, replica_groups=mesh['dp'=8,'mp'=4] {'dp'}, dimensions={1}, use_global_device_ids=true | all-gather | bytes 589824 | tf_op jit(solution)/shard_map/all_gather | solution.py:111
  106.8 28.6 %scatter_custom_fusion.1 = bf16[8192]{0:T(1024)(128)(2,1)S(1)} fusion(s32[4096]{0:T(1024)S(1)} %bitcast.245, bf16[4096]{0:T(1024)(128)(2,1)S(1)} %broadcast.185, bf16[]{:T(256)} %constant.92.clone.1), kind=kCustom, calls=%fused_computation.174 | custom fusion | bytes 16386 | tf_op jit(solution)/shard_map/scatter | solution.py:104
  135.4 15.8 %scatter_custom_fusion = s32[8192]{0:T(1024)S(1)} fusion(s32[4096]{0:T(1024)S(1)} %bitcast.246, s32[4096]{0:T(1024)S(1)} %iota.19, s32[]{:T(128)} %constant.91.clone.1), kind=kCustom, calls=%fused_computation.170 | custom fusion | bytes 32772 | tf_op jit(solution)/shard_map/scatter | solution.py:102
  159.7 33.7 %gather_fusion = bf16[8192,512]{1,0:T(8,128)(2,1)} fusion(bf16[2048,512]{1,0:T(8,128)(2,1)S(1)} %fusion.57, s32[8192]{0:T(1024)S(1)} %get-tuple-element.221), kind=kCustom, calls=%fused_computation | custom fusion | bytes 16809984 | tf_op jit(solution)/shard_map/gather | solution.py:106
  199.8 12.1 gather_fusion.1
  216.2 226.7 %while.26 = (s32[]{:T(128)}, bf16[8,512,64]{1,2,0:T(8,128)(2,1)}, f32[8,512]{1,0:T(8,128)}, bf16[8,512,64]{2,1,0:T(8,128)(2,1)S(1)}, bf16[8192,64]{1,0:T(8,128)(...) while((s32[]{:T(128)}, bf16[8,512,64]{1,2,0:T(8,128)(2,1)}, ...), condition=%wide.region_12.13_spmd.clone, body=%wide.region_9.12_spmd.clone.sunk | while | flops 1124113920 | bytes 54775924 | solution.py:148
  445.8 29.5 %gather_fusion.2 = bf16[8192,64]{1,0:T(8,128)(2,1)} fusion(bf16[4096,64]{1,0:T(8,128)(2,1)S(1)} %bitcast.214, s32[8192]{0:T(1024)S(1)} %copy-done.27), kind=kCustom, calls=%fused_computation.2 | custom fusion | bytes 2129920 | tf_op jit(solution)/shard_map/gather | solution.py:150
  484.2 21.9 %gather_fusion.3 = bf16[4096,512]{1,0:T(8,128)(2,1)} fusion(bf16[8192,512]{1,0:T(8,128)(2,1)} %bitcast.217, s32[4096]{0:T(1024)S(1)} %copy-done.31), kind=kCustom, calls=%fused_computation.3 | custom fusion | bytes 8404992 | tf_op jit(solution)/shard_map/gather | solution.py:161
  513.5 16.0 %fusion.129 = f32[2048,1,512]{2,1,0:T(1,128)S(1)} fusion(f32[2048,2,1]{1,2,0:T(1,128)S(1)} %bitcast.233, bf16[2048,2,512]{2,1,0:T(2,128)(2,1)} %reshape.253), kind=kOutput, calls=%fused_computation.196 | convolution fusion | flops 25165824 | bytes 8404992 | tf_op jit(solution)/shard_map/ts,tsd->td/dot_general | solution.py:162
  532.9 14.8 %multiply_convert_fusion.1 = (bf16[2048,2048]{1,0:T(8,128)(2,1)}, f32[2048,2048]{1,0:T(8,128)}) fusion(f32[2048]{0:T(1024)S(1)} %bitcast.248, bf16[512,2048]{1,0:T(8,128)(2,1)} %all-gather.7.cloned.1.call-done, f32[2048,512]{1,0:T(8,128)} %copy-done.14, f32[512]{0:T(512)S(1)} %copy-done.66, f32[512]{0:T(512)S(1)} %copy-done.59, ...), kind=kOutput, calls=%fused_computation.63 | convolution fusion | flops 4342153216 | bytes 31485952 | tf_op jit(solution)/shard_map/dot_general | solution.py:166
  547.7 19.1 %fusion.127 = (bf16[2048]{0:T(1024)(128)(2,1)}, bf16[2048,2048]{1,0:T(8,128)(2,1)}) fusion(f32[2048,2048]{1,0:T(8,128)} %get-tuple-element.223, f32[2048]{0:T(1024)S(1)} %bitcast.249, bf16[2048,512]{1,0:T(8,128)(2,1)} %all-gather.9.cloned.1.call-done, bf16[1,2048,512]{2,1,0:T(8,128)(2,1)S(1)} %copy-done.20), kind=kOutput, calls=%fused_computation.194 | convolution fusion | flops 4387239936 | bytes 29372416 | tf_op jit(solution)/shard_map/td,fd->tf/dot_general | solution.py:180
  600.2 36.7 %gather_fusion.4 = bf16[8192,512]{1,0:T(8,128)(2,1)} fusion(bf16[4096,512]{1,0:T(8,128)(2,1)} %multiply_convert_fusion.2, s32[8192]{0:T(1024)S(1)} %copy-done.27), kind=kCustom, calls=%fused_computation.4 | custom fusion | bytes 16809984 | tf_op jit(solution)/shard_map/gather | solution.py:205
  648.1 13.0 gather_fusion.5
  661.2 422.8 %while.27 = (s32[]{:T(128)}, f32[8192,128]{0,1:T(8,128)}, bf16[8,512,64]{1,2,0:T(8,128)(2,1)}, bf16[8,512,64]{2,1,0:T(8,128)(2,1)}, bf16[8192,64]{1,0:T(8,128)(2...) while((s32[]{:T(128)}, f32[8192,128]{0,1:T(8,128)}, ...), condition=%wide.region_19.20_spmd.clone, body=%wide.region_17.19_spmd.clone.sunk | while | flops 2725813760 | bytes 264923504 | solution.py:241
  683.7 11.6 multiply_convert_fusion.4
  1085.5 24.0 %gather_fusion.6 = bf16[8192,64]{1,0:T(8,128)(2,1)S(1)} fusion(bf16[4096,64]{1,0:T(8,128)(2,1)S(1)} %bitcast.215, s32[8192]{0:T(1024)S(1)} %copy-done.28), kind=kCustom, calls=%fused_computation.6 | custom fusion | bytes 2129920 | tf_op jit(solution)/shard_map/gather | solution.py:256
  1122.4 20.5 %fusion.69 = f32[2048,1,2]{2,1,0:T(1,128)S(1)} fusion(bf16[2048,2,512]{2,1,0:T(2,128)(2,1)} %reshape.253, f32[2048,512,1]{1,0,2:T(8,128)} %bitcast.220), kind=kOutput, calls=%fused_computation.105 | convolution fusion | flops 25165824 | bytes 8404992 | tf_op jit(solution)/shard_map/td,tsd->ts/dot_general | solution.py:193
  1145.0 14.1 fusion.131
  1199.6 22.2 %gather_fusion.7 = bf16[4096,512]{1,0:T(8,128)(2,1)} fusion(bf16[8192,512]{1,0:T(8,128)(2,1)} %bitcast.216, s32[4096]{0:T(1024)S(1)} %copy-done.32), kind=kCustom, calls=%fused_computation.7 | custom fusion | bytes 8404992 | tf_op jit(solution)/shard_map/gather | solution.py:276
  1231.5 15.5 %reduce_sum.206 = f32[2048,512]{1,0:T(8,128)} reduce(f32[2048,2,512]{2,1,0:T(2,128)} %reshape.259, f32[]{:T(128)} %constant.54.clone.1), dimensions={1}, to_apply=%region_20.21 | reduce | flops 1048576 | bytes 12582916 | tf_op jit(solution)/shard_map/reduce_sum | solution.py:277
  1294.6 34.2 %reduce-scatter.18.cloned.1.call-done = bf16[512,512]{1,0:T(8,128)(2,1)} async-done(((bf16[512,2048]{1,0:T(8,128)(2,1)}), bf16[512,512]{1,0:T(8,128)(2,1)}) %reduce-scatter.18.cloned.1.call-update) | async-done | bytes 524304 | tf_op jit(solution)/shard_map/reduce_scatter | solution.py:289
  1328.9 22.3 %reduce-scatter.12.cloned.1.call-done = bf16[128,128]{1,0:T(8,128)(2,1)} async-done(((bf16[512,128]{1,0:T(8,128)(2,1)}), bf16[128,128]{1,0:T(8,128)(2,1)}) %reduce-scatter.12.cloned.1.call-update) | async-done | bytes 32784 | tf_op jit(solution)/shard_map/reduce_scatter | solution.py:301
  1351.2 95.8 %all-reduce.9 = (f32[128]{0:T(128)}, f32[128]{0:T(128)}, f32[128,8]{0,1:T(8,128)}, f32[128,128]{1,0:T(8,128)}, f32[128]{0:T(128)}, /*index=5*/f32[128]{0:T(128)}...) all-reduce(f32[128]{0:T(128)S(1)} %dynamic-slice_convert_fusion.5, ...), channel_id=1, replica_groups=mesh['dp'=8,'mp'=4] {'dp'}, use_global_device_ids=true, to_apply=%region_27.28 | all-reduce | flops 542848 | bytes 3259392 | tf_op jit(solution)/shard_map/psum | solution.py:320
  (482 shorter events, 868.4 us)
Async XLA Ops:
  7.2 204.7 %all-gather.5.cloned.1.call-start = ((), (), s32[]{:S(2)}) async-start(), calls=%async_computation.8 | async-start | bytes 2621440 | tf_op jit(solution)/shard_map/all_gather | solution.py:85
  12.9 146.8 %copy-start.2 = (bf16[2048,512]{1,0:T(8,128)(2,1)}, bf16[2048,512]{1,0:T(8,128)(2,1)S(1)}, u32[]{:S(2)}) copy-start(bf16[2048,512]{1,0:T(8,128)(2,1)S(1)} %fusion.57) | copy-start | bytes 6291460
  14.5 518.4 %all-gather.7.cloned.1.call-start = ((), (), s32[]{:S(2)}) async-start(), calls=%async_computation.9 | async-start | bytes 2621440 | tf_op jit(solution)/shard_map/all_gather | solution.py:88
  15.2 532.4 %all-gather.9.cloned.1.call-start = ((), (), s32[]{:S(2)}) async-start(), calls=%async_computation.10 | async-start | bytes 2621440 | tf_op jit(solution)/shard_map/all_gather | solution.py:90
  16.9 137.2 %copy-start.48 = (bf16[512,8]{0,1:T(8,128)(2,1)S(1)}, bf16[512,8]{0,1:T(8,128)(2,1)}, u32[]{:S(2)}) copy-start(bf16[512,8]{0,1:T(8,128)(2,1)} %param.25) | copy-start | bytes 24580
  106.7 93.0 %copy-start.30 = (s32[4096]{0:T(1024)}, s32[4096]{0:T(1024)S(1)}, u32[]{:S(2)}) copy-start(s32[4096]{0:T(1024)S(1)} %broadcast_clamp_fusion) | copy-start | bytes 49156
  135.4 58.0 %copy-start.38 = (bf16[8,1024]{1,0:T(8,128)(2,1)}, bf16[8,1024]{1,0:T(8,128)(2,1)S(1)}, u32[]{:S(2)}) copy-start(bf16[8,1024]{1,0:T(8,128)(2,1)S(1)} %mul.238) | copy-start | bytes 49156
  155.1 38.2 %copy-start.16 = (f32[2048,2]{1,0:T(8,128)}, f32[2048,2]{1,0:T(8,128)S(1)}, u32[]{:S(2)}) copy-start(f32[2048,2]{1,0:T(8,128)S(1)} %copy.87) | copy-start | bytes 49156
  155.2 38.2 %copy-start.36 = (f32[2048]{0:T(1024)}, f32[2048]{0:T(1024)S(1)}, u32[]{:S(2)}) copy-start(f32[2048]{0:T(1024)S(1)} %reduce_max.18) | copy-start | bytes 24580
  155.8 37.5 %copy-start.41 = (f32[2048]{0:T(1024)}, f32[2048]{0:T(1024)S(1)}, u32[]{:S(2)}) copy-start(f32[2048]{0:T(1024)S(1)} %fusion.93) | copy-start | bytes 24580
  216.2 229.6 %copy-start.27 = (s32[8192]{0:T(1024)S(1)}, s32[8192]{0:T(1024)}, u32[]{:S(2)}) copy-start(s32[8192]{0:T(1024)} %get-tuple-element.220) | copy-start | bytes 98308
  443.9 31.4 %copy-start.4 = (bf16[8192,64]{1,0:T(8,128)(2,1)}, bf16[8192,64]{1,0:T(8,128)(2,1)S(1)}, u32[]{:S(2)}) copy-start(bf16[8192,64]{1,0:T(8,128)(2,1)S(1)} %get-tuple-element.406) | copy-start | bytes 3145732
  445.8 31.8 %copy-start.39 = (bf16[8,1024]{1,0:T(8,128)(2,1)S(1)}, bf16[8,1024]{1,0:T(8,128)(2,1)}, u32[]{:S(2)}) copy-start(bf16[8,1024]{1,0:T(8,128)(2,1)} %copy-done.38) | copy-start | bytes 49156
  530.0 45.6 %copy-start.45 = (f32[2048]{0:T(1024)}, f32[2048]{0:T(1024)S(1)}, u32[]{:S(2)}) copy-start(f32[2048]{0:T(1024)S(1)} %broadcast_multiply_fusion.5) | copy-start | bytes 24580
  532.8 42.8 %copy-start.50 = (f32[2048]{0:T(1024)}, f32[2048]{0:T(1024)S(1)}, u32[]{:S(2)}) copy-start(f32[2048]{0:T(1024)S(1)} %add_rsqrt_fusion) | copy-start | bytes 24580
  661.2 424.3 %copy-start.28 = (s32[8192]{0:T(1024)S(1)}, s32[8192]{0:T(1024)}, u32[]{:S(2)}) copy-start(s32[8192]{0:T(1024)} %get-tuple-element.220) | copy-start | bytes 98308
  1116.4 44.6 %all-to-all-start = ((bf16[8,128,512]{2,1,0:T(8,128)(2,1)}), bf16[8,128,512]{2,1,0:T(8,128)(2,1)}, u32[]{:S(2)}, u32[]{:S(2)}) async-start(bf16[8,128,512]{2,1,0:T(8,128)(2,1)} %maximum_bitcast_fusion), calls=%async_computation.2 | async-start | bytes 2097152 | tf_op jit(solution)/shard_map/all_to_all | solution.py:19
  1122.3 135.7 %reduce-scatter.22.cloned.1.call-start = ((), (), s32[]{:S(2)}) async-start(), calls=%async_computation.17 | async-start | bytes 163840
  1161.0 97.9 %reduce-scatter.14.cloned.1.call-start = ((), (), s32[]{:S(2)}) async-start(), calls=%async_computation.13 | async-start | bytes 81920 | tf_op jit(solution)/shard_map/reduce_scatter | solution.py:283
  1163.1 97.1 %reduce-scatter.16.cloned.1.call-start = ((), (), s32[]{:S(2)}) async-start(), calls=%async_computation.14 | async-start | bytes 81920 | tf_op jit(solution)/shard_map/reduce_scatter | solution.py:286
  1163.6 97.9 %reduce-scatter.10.cloned.1.call-start = ((), (), s32[]{:S(2)}) async-start(), calls=%async_computation.11 | async-start | bytes 2621440 | tf_op jit(solution)/shard_map/reduce_scatter | solution.py:246
  1167.5 127.1 %reduce-scatter.20.cloned.1.call-start = ((), (), s32[]{:S(2)}) async-start(), calls=%async_computation.16 | async-start | bytes 2621440 | tf_op jit(solution)/shard_map/reduce_scatter | solution.py:295
  1177.8 151.0 %reduce-scatter.18.cloned.1.call-start = ((), (), s32[]{:S(2)}) async-start(), calls=%async_computation.15 | async-start | bytes 2621440 | tf_op jit(solution)/shard_map/reduce_scatter | solution.py:289
  1188.7 162.5 %reduce-scatter.12.cloned.1.call-start = ((), (), s32[]{:S(2)}) async-start(), calls=%async_computation.12 | async-start | bytes 163840 | tf_op jit(solution)/shard_map/reduce_scatter | solution.py:301
  (105 other events, 733.0 us)
Sparse Core Ops, SparseCore 0:
  14.6 25.9 all-gather.4
  42.2 22.5 all-gather.6
  66.4 22.5 all-gather.8
  1161.1 21.1 reduce-scatter.21
  1184.6 19.4 reduce-scatter.13
  1206.9 19.4 reduce-scatter.15
  1229.1 31.4 reduce-scatter.9
  1263.1 31.4 reduce-scatter.19
  1297.3 31.4 reduce-scatter.17
  1331.6 19.5 reduce-scatter.11
where the time goes:
time: 1470 us; the launch traced here: 1450 us
  matrix products  564 us (38%)
  local copies, waits for them, and re-layouts  364 us (25%)
  other arithmetic  248 us (17%)
  blocking collectives  186 us (13%)
  waiting for transfers between devices  68.1 us (5%)
  between operations  17.1 us (1%)
    dot_general x16, matrix products, scores_of(): jnp.einsum('qh,kh->qk', query_block, keys, preferred_element_type=jnp.flo...  149 us
    psum x1, blocking collectives, on_device(): lax.psum((shares[2], shares[3], shares[4], shares[5], shares[6], shares[7...  95.8 us
    convert_element_type x8, other arithmetic, attend_back(): scores_grad = (attention * (attention_grad - delta)).astype(jnp.bfloat16)  92.7 us
    reduce_sum x8, other arithmetic, attend(): total = jnp.sum(weights, axis=1, keepdims=True)  78.2 us
    dot_general x8, matrix products, attend_back(): jnp.einsum('qh,kh->qk', grad_block, value_rows, preferred_element_type=jn...  77.2 us
    dot_general x8, matrix products, attend(): jnp.dot(attention, value_rows, preferred_element_type=jnp.float32)  74.8 us
    while x112, local copies, waits for them, and re-layouts  47.7 us
    dot_general x8, matrix products, attend_back(): jnp.dot(scores_grad, keys, preferred_element_type=jnp.float32) * score_scale  39 us
  transfers between devices with their start and end apart: 11, of which 3 were waited for; matrix products, arithmetic and copies ran while one was open for 41% of the time, Pallas kernels for 0%

commit v1 on v0

v1 whole, which is shorter than its diff:
```python
import functools

import jax
import jax.numpy as jnp
from jax import lax
from jax.experimental import pallas as pl
from jax.experimental.pallas import tpu as pltpu
from jax.sharding import PartitionSpec as P

F32 = jnp.float32
BF = jnp.bfloat16
EPS = 1e-05
LOG2E = 1.4426950408889634
LN2 = 0.6931471805599453
MASKED = -1e30
GELU_A = 0.7978845608028654
GELU_B = 0.044715
SAFE = 50.0
LANES = 128


def nn(a, b):
    return lax.dot_general(a, b, (((1,), (0,)), ((), ())), preferred_element_type=F32)


def nt(a, b):
    return lax.dot_general(a, b, (((1,), (1,)), ((), ())), preferred_element_type=F32)


def tn(a, b):
    return lax.dot_general(a, b, (((0,), (0,)), ((), ())), preferred_element_type=F32)


def norm_parts(values):
    centred = values - jnp.mean(values, axis=-1, keepdims=True)
    inverse = lax.rsqrt(jnp.mean(centred * centred, axis=-1, keepdims=True) + EPS)
    return centred * inverse, inverse


def norm_back(grad, normal, inverse, gain):
    scaled = grad * gain
    return inverse * (
        scaled
        - jnp.mean(scaled, axis=-1, keepdims=True)
        - normal * jnp.mean(scaled * normal, axis=-1, keepdims=True)
    )


def three(value):
    high = value.astype(BF).astype(F32)
    rest = value - high
    middle = rest.astype(BF).astype(F32)
    return high, middle, rest - middle


def extra_rows(value, last):
    row = lax.broadcasted_iota(jnp.int32, (16, value.shape[1]), 0)
    high, middle, low = three(value)
    out = jnp.where(row == 0, -high, 0.0)
    out = jnp.where(row == 1, -middle, out)
    out = jnp.where(row == 2, -low, out)
    return jnp.where(row == 3, last, out)


def spread(first, second, route0, route1, experts):
    zero = jnp.zeros_like(first)
    return jnp.concatenate(
        [
            jnp.where(route0 == e, first, jnp.where(route1 == e, second, zero))
            for e in range(experts)
        ],
        axis=0,
    )


def picked(table, route, experts):
    head = table.shape[0] // experts
    out = jnp.zeros((head, table.shape[1]), F32)
    for e in range(experts):
        out = jnp.where(route == e, table[e * head : (e + 1) * head, :], out)
    return out


def key_rows(pair, live, head):
    lane = lax.broadcasted_iota(jnp.int32, pair.shape, 1)
    row = lax.broadcasted_iota(jnp.int32, pair.shape, 0)
    ones = jnp.where(lane < head + 3, 1.0, 0.0)
    mask = jnp.where(row < live, 0.0, MASKED)
    out = jnp.where(lane == head + 3, mask, ones)
    return jnp.where(lane < head, pair.astype(F32), out).astype(BF)


def first_kernel(x, gain, bias, router, proj, routes, normed, pairs, gates):
    experts = router.shape[0] // 2
    normal, _ = norm_parts(x[...].astype(F32))
    out = (normal * gain[...] + bias[...]).astype(BF)
    normed[...] = out
    pairs[...] = nn(out, proj[...]).astype(BF)
    logits = nt(router[...], out)
    route = routes[...]
    chosen = []
    for s in range(2):
        one = jnp.zeros((1, logits.shape[1]), F32)
        for e in range(experts):
            one = jnp.where(route[s : s + 1, :] == e, logits[e : e + 1, :], one)
        chosen.append(one)
    top = jnp.maximum(chosen[0], chosen[1])
    up0, up1 = jnp.exp(chosen[0] - top), jnp.exp(chosen[1] - top)
    inverse = 1.0 / (up0 + up1)
    gates[0:1, :] = up0 * inverse
    gates[1:2, :] = up1 * inverse


def query_kernel(normed, table, routes, queries, *, experts, scale):
    every = nt(table[...], normed[...]) * scale
    for s in range(2):
        queries[s] = picked(every, routes[s : s + 1, :], experts).astype(BF)


def attend_kernel(live, q, p0, p1, p2, p3, out, keys, values, limit, top, *, head, span):
    part = p0.shape[0]

    @pl.when((pl.program_id(0) == 0) & (pl.program_id(1) == 0))
    def _():
        row = lax.broadcasted_iota(jnp.int32, (LANES, LANES), 0)
        col = lax.broadcasted_iota(jnp.int32, (LANES, LANES), 1)
        move = jnp.where((col == row + head) & (row < head), 1.0, 0.0).astype(BF)
        count = jnp.where(row < head, 1.0, 0.0).astype(BF)
        longest = jnp.zeros((1, LANES), F32)
        for o, p in enumerate((p0, p1, p2, p3)):
            pair = p[...]
            keys[o * part : (o + 1) * part, :] = key_rows(pair, live[o], head)
            turned = nt(move, pair)
            line = lax.broadcasted_iota(jnp.int32, turned.shape, 0)
            values[:, o * part : (o + 1) * part] = jnp.where(line == head, 1.0, turned).astype(BF)
            wide = pair.astype(F32)
            squares = nn((wide * wide).astype(BF), count)
            longest = jnp.maximum(longest, jnp.max(squares, axis=0, keepdims=True))
        limit[...] = jnp.broadcast_to(1.02 * jnp.sqrt(longest), limit.shape)

    query = q[0]
    wide = query.astype(F32)
    length = jnp.sqrt(jnp.sum(wide * wide, axis=0, keepdims=True))
    bound = length * limit[0:1, 0:1]
    top[...] = jnp.broadcast_to(bound, top.shape)
    n = query.shape[1]
    rest = jnp.zeros((LANES - head - 16, n), BF)

    @pl.when(jnp.max(bound) > SAFE)
    def _():
        plain = jnp.concatenate(
            [query, extra_rows(jnp.zeros((1, n), F32), 1.0).astype(BF), rest], axis=0
        )

        def peak(j, now):
            at = pl.multiple_of(j * 512, 512)
            scores = nn(keys[pl.ds(at, 512), :], plain)
            return jnp.maximum(now, jnp.max(scores, axis=0, keepdims=True))

        best = lax.fori_loop(0, 4 * part // 512, peak, jnp.full((1, n), -3e38, F32))
        top[...] = jnp.broadcast_to(best, top.shape)

    peak_row = top[0:1, :]
    extended = jnp.concatenate([query, extra_rows(peak_row, 1.0).astype(BF), rest], axis=0)
    total = jnp.zeros((LANES, n), F32)
    for j in range(4 * part // span):
        here = slice(j * span, (j + 1) * span)
        weights = jnp.exp2(nn(keys[here, :], extended)).astype(BF)
        total = total + nn(values[:, here], weights)
    weight = total[head : head + 1, :]
    out[0, 0:head, :] = total[0:head, :] / weight
    out[0, head : head + 8, :] = jnp.broadcast_to(peak_row + jnp.log2(weight), (8, n))


def attend_back_kernel(live, q, do, qt, dot, pair, before, after, grads, keys, values, kt, vt, *, head, tile):
    step = pl.program_id(0)
    part = pair.shape[0]

    @pl.when(step == 0)
    def _():
        rows = pair[...]
        keys[...] = key_rows(rows, live[0], head)
        lane = lax.broadcasted_iota(jnp.int32, rows.shape, 1)
        fixed = jnp.where(lane < 3, 1.0, 0.0)
        values[...] = jnp.where(lane < head, fixed, rows.astype(F32)).astype(BF)
        kt[...] = jnp.zeros_like(kt)
        vt[...] = jnp.zeros_like(vt)

    attention = jnp.exp2(nt(q[0], keys[...]))
    pull = nt(do[0], values[...])
    scores = (attention * pull).astype(BF)
    kt[...] += nn(qt[0], scores)
    vt[...] += nn(dot[0], attention.astype(BF))
    after[0] = before[0] + nn(scores, keys[...])

    @pl.when(step == pl.num_programs(0) - 1)
    def _():
        grads[0:head, :] = (kt[...] * LN2).astype(BF)
        grads[head : 2 * head, :] = vt[...].astype(BF)


def middle_kernel(
    att, qt, routes, gates, x, up, normed,
    we0, we1, we2, we3, eb, wr0, wr1, wr2, wr3, rb, gain, bias, wo,
    out, mid_grad, q_rows, do_rows, do_t, logit, g0, g1, g2, g3, wo_grad,
    we_sum, wr_sum, wo_sum, eb_sum, small, rt_sum,
    *, head, experts,
):
    step = pl.program_id(0)

    @pl.when(step == 0)
    def _():
        for r in (we_sum, wr_sum, wo_sum, eb_sum, small, rt_sum):
            r[...] = jnp.zeros_like(r)

    route0, route1 = routes[0:1, :], routes[1:2, :]
    gate0, gate1 = gates[0:1, :], gates[1:2, :]
    mix0, mix1 = att[0, 0:head, :], att[1, 0:head, :]
    low0, low1 = mix0.astype(BF).astype(F32), mix1.astype(BF).astype(F32)
    mixed = spread(gate0 * low0, gate1 * low1, route0, route1, experts).astype(BF)
    middle = x[...].astype(F32) + tn(mixed, wo[...])
    normal, inverse = norm_parts(middle)
    normed_two = (normal * gain[...] + bias[...]).astype(BF)
    upstream = up[...]
    n2t = normed_two.T
    upt = upstream.T
    ff = we0.shape[1]
    reduced = jnp.zeros(middle.shape, F32)
    two_grad = jnp.zeros(middle.shape, F32)
    for o, (we, wr) in enumerate(((we0, wr0), (we1, wr1), (we2, wr2), (we3, wr3))):
        here = slice(o * ff, (o + 1) * ff)
        v = nn(normed_two, we[...]) + eb[o : o + 1, :]
        square = v * v
        inner = v * (GELU_A + (GELU_A * GELU_B) * square)
        half = 0.5 + 0.5 * jnp.tanh(inner)
        act = v * half
        slope = half + 2.0 * act * (1.0 - half) * (GELU_A + (3.0 * GELU_A * GELU_B) * square)
        low = act.astype(BF)
        reduced = reduced + nn(low, wr[...])
        back = nt(upstream, wr[...]) * slope
        back_low = back.astype(BF)
        two_grad = two_grad + nt(back_low, we[...])
        we_sum[:, here] += nn(n2t, back_low)
        wr_sum[:, here] += nn(upt, low)
        eb_sum[0:1, here] += jnp.sum(back_low.astype(F32), axis=0, keepdims=True)
    out[...] = (middle + reduced + rb[...]).astype(BF)
    wide_up = upstream.astype(F32)
    mid = wide_up + norm_back(two_grad, normal, inverse, gain[...])
    mid_grad[...] = mid
    small[0:1, :] += jnp.sum(wide_up, axis=0, keepdims=True)
    small[1:2, :] += jnp.sum(two_grad * normal, axis=0, keepdims=True)
    small[2:3, :] += jnp.sum(two_grad, axis=0, keepdims=True)
    mid_low = mid.astype(BF)
    wo_sum[...] += nn(mixed, mid_low)
    every = nt(wo[...], mid_low)
    pull0, pull1 = picked(every, route0, experts), picked(every, route1, experts)
    gate_grad0 = jnp.sum(low0 * pull0, axis=0, keepdims=True)
    gate_grad1 = jnp.sum(low1 * pull1, axis=0, keepdims=True)
    both = gate0 * gate_grad0 + gate1 * gate_grad1
    chosen0, chosen1 = gate0 * (gate_grad0 - both), gate1 * (gate_grad1 - both)
    row = lax.broadcasted_iota(jnp.int32, (16, chosen0.shape[1]), 0)
    logit_rows = jnp.where(row == route0, chosen0, jnp.where(row == route1, chosen1, 0.0))
    logit_high = logit_rows.astype(BF)
    logit_low = (logit_rows - logit_high.astype(F32)).astype(BF)
    logit[...] = logit_high
    here_normed = normed[...]
    rt_sum[...] += nn(logit_high, here_normed) + nn(logit_low, here_normed)
    rest = jnp.zeros((LANES - head - 16, row.shape[1]), F32)
    for s, (gate, pull, mix) in enumerate(((gate0, pull0, mix0), (gate1, pull1, mix1))):
        grad_low = (gate * pull).astype(BF)
        do_t[s] = grad_low
        grad = grad_low.astype(F32)
        delta = jnp.sum(grad * mix, axis=0, keepdims=True)
        do_rows[s] = jnp.concatenate([extra_rows(delta, 0.0), rest, grad], axis=0).T.astype(BF)
        total = att[s, head : head + 1, :]
        query = qt[s].astype(F32)
        q_rows[s] = jnp.concatenate([query, extra_rows(total, 1.0), rest], axis=0).T.astype(BF)

    @pl.when(step == pl.num_programs(0) - 1)
    def _():
        wo_grad[...] = wo_sum[...].astype(BF)
        width = we_sum.shape[0]
        for o, g in enumerate((g0, g1, g2, g3)):
            here = slice(o * ff, (o + 1) * ff)
            g[0:width, :] = we_sum[:, here].astype(BF)
            g[width : 2 * width, :] = wr_sum[:, here].astype(BF)
            line = lax.broadcasted_iota(jnp.int32, (8, ff), 0)
            head_rows = jnp.where(line == 3, eb_sum[0:1, here], small[...])
            g[2 * width : 2 * width + 16, :] = jnp.concatenate(
                [head_rows, rt_sum[0:8, :]], axis=0
            ).astype(BF)
            g[2 * width + 16 :, :] = jnp.zeros((g.shape[0] - 2 * width - 16, ff), BF)


def last_kernel(
    where, dq, pa, pb, pc, logit, routes, normed, x, mid_grad, gain, wq, proj, router,
    out, q0, q1, q2, q3, s0, s1, s2, s3, wq_sum, sp_sum, small, *, head, experts, scale,
):
    step = pl.program_id(0)

    @pl.when(step == 0)
    def _():
        for r in (wq_sum, sp_sum, small):
            r[...] = jnp.zeros_like(r)

    route0, route1 = routes[0:1, :], routes[1:2, :]
    grad0 = (dq[0].T)[0:head, :] * scale
    grad1 = (dq[1].T)[0:head, :] * scale
    placed = spread(grad0, grad1, route0, route1, experts).astype(BF)
    pair = (pa[...].astype(F32) + pb[...].astype(F32) + pc[...].astype(F32)).astype(BF)
    normed_grad = tn(placed, wq[...]) + tn(pair, proj[...]) + tn(logit[...], router[...])
    here_normed = normed[...]
    wq_sum[...] += nn(placed, here_normed)
    sp_sum[...] += nn(pair, here_normed)
    normal, inverse = norm_parts(x[...].astype(F32))
    out[...] = mid_grad[...] + norm_back(normed_grad, normal, inverse, gain[...])
    small[0:1, :] += jnp.sum(normed_grad * normal, axis=0, keepdims=True)
    small[1:2, :] += jnp.sum(normed_grad, axis=0, keepdims=True)

    @pl.when(step == pl.num_programs(0) - 1)
    def _():
        share = head // 4
        block = sp_sum.shape[1] // 4
        for o, (q, s) in enumerate(((q0, s0), (q1, s1), (q2, s2), (q3, s3))):
            owner = where[o]
            for e in range(experts):
                at = pl.multiple_of(e * head + owner * share, share)
                q[e * share : (e + 1) * share, :] = wq_sum[pl.ds(at, share), :].astype(BF)
            lanes = pl.ds(pl.multiple_of(owner * block, block), block)
            wide = sp_sum.shape[0]
            s[0:wide, :] = sp_sum[:, lanes].astype(BF)
            s[wide : wide + 16, :] = jnp.concatenate(
                [small[:, lanes], jnp.zeros((8, block), F32)], axis=0
            ).astype(BF)


def swapped(value, bit):
    return lax.ppermute(value, "mp", [(i, i ^ bit) for i in range(4)])


def four(value):
    across = swapped(value, 2)
    return value, swapped(value, 1), across, swapped(across, 1)


def summed(a, b):
    return (a.astype(F32) + b.astype(F32)).astype(BF)


def group_sum(parts):
    far = summed(parts[2], swapped(parts[3], 1))
    near = summed(parts[0], swapped(parts[1], 1))
    return near, swapped(far, 2)


def sent_to_all(value, axes):
    n = lax.axis_size(axes)
    wide = jnp.broadcast_to(value[None], (n,) + value.shape)
    return lax.all_to_all(wide, axes, split_axis=0, concat_axis=0, tiled=True)


def whole_table(share, experts):
    dp, mp = lax.axis_size("dp"), lax.axis_size("mp")
    rows, cols = share.shape
    every = sent_to_all(share, ("dp", "mp"))
    each = every.reshape(experts, dp // experts, mp, rows, cols)
    return each.transpose(0, 2, 3, 1, 4).reshape(experts * mp * rows, dp // experts * cols)


def spec(shape, index):
    return pl.BlockSpec(shape, index)


def fixed(shape):
    return pl.BlockSpec(shape, lambda *_: (0,) * len(shape))


def shape(dims, kind):
    return jax.ShapeDtypeStruct(dims, kind)


SMEM = pl.BlockSpec(memory_space=pltpu.SMEM)
PARAMS = pltpu.CompilerParams(vmem_limit_bytes=58 * 2**20)


def on_device(
    block_input, routes, lengths, first_gain, first_bias, router_weight, shared_proj,
    query_weight, output_weight, second_gain, second_bias, expand_weight, expand_bias,
    reduce_weight, reduce_bias, upstream_grad,
):
    tokens, width = block_input.shape[1], block_input.shape[2]
    experts = router_weight.shape[1]
    head = query_weight.shape[0] * lax.axis_size("mp")
    dp = lax.axis_size("dp")
    units = expand_weight.shape[1]
    me = lax.axis_index("mp")
    owners = me ^ jnp.arange(4, dtype=jnp.int32)
    live = jnp.clip(lengths[0] - owners * tokens, 0, tokens)
    x = block_input.reshape(tokens, width)
    up = upstream_grad.reshape(tokens, width)
    routes_t = routes.reshape(tokens, 2).T
    router_t = jnp.concatenate([router_weight.T, jnp.zeros((experts, width), BF)], axis=0)
    gain1, bias1 = first_gain[None], first_bias[None]
    gain2, bias2 = second_gain[None], second_bias[None]

    wq = whole_table(query_weight, experts)

    tb = 512
    rows = spec((tb, width), lambda i: (i, 0))
    cols2 = spec((2, tb), lambda i: (0, i))
    normed, pairs, gates = pl.pallas_call(
        first_kernel,
        grid=(tokens // tb,),
        in_specs=[rows, fixed((1, width)), fixed((1, width)), fixed((2 * experts, width)),
                  fixed((width, 2 * head)), cols2],
        out_specs=[rows, spec((tb, 2 * head), lambda i: (i, 0)), cols2],
        out_shape=[shape((tokens, width), BF), shape((tokens, 2 * head), BF), shape((2, tokens), F32)],
        compiler_params=PARAMS,
    )(x, gain1, bias1, router_t, shared_proj, routes_t)

    pair = four(pairs)
    queries = pl.pallas_call(
        functools.partial(query_kernel, experts=experts, scale=0.125 * LOG2E),
        grid=(tokens // tb,),
        in_specs=[rows, fixed((experts * head, width)), cols2],
        out_specs=spec((2, head, tb), lambda i: (0, 0, i)),
        out_shape=shape((2, head, tokens), BF),
        compiler_params=PARAMS,
    )(normed, wq, routes_t)

    queries, ow, ew, rw, eb = lax.optimization_barrier(
        (queries, output_weight, expand_weight, reduce_weight, expand_bias)
    )
    wo = whole_table(ow, experts)
    wes, wrs = four(ew), four(rw)
    ebs = jnp.concatenate(four(eb[None]), axis=0).astype(F32)

    tq = 512
    att = pl.pallas_call(
        functools.partial(attend_kernel, head=head, span=4 * tokens),
        grid=(2, tokens // tq),
        in_specs=[SMEM, spec((1, head, tq), lambda s, i: (s, 0, i))] + [fixed((tokens, 2 * head))] * 4,
        out_specs=spec((1, head + 8, tq), lambda s, i: (s, 0, i)),
        out_shape=shape((2, head + 8, tokens), F32),
        scratch_shapes=[
            pltpu.VMEM((4 * tokens, LANES), BF), pltpu.VMEM((LANES, 4 * tokens), BF),
            pltpu.VMEM((8, LANES), F32), pltpu.VMEM((8, tq), F32),
        ],
        compiler_params=PARAMS,
    )(live, queries, *pair)

    tm = 256
    rows = spec((tm, width), lambda i: (i, 0))
    cols2 = spec((2, tm), lambda i: (0, i))
    tail = 1152
    both_rows = spec((2, tm, LANES), lambda i: (0, i, 0))
    both_cols = spec((2, head, tm), lambda i: (0, 0, i))
    block_out, mid_grad, q_rows, do_rows, do_t, logit, *grads = pl.pallas_call(
        functools.partial(middle_kernel, head=head, experts=experts),
        grid=(tokens // tm,),
        in_specs=[spec((2, head + 8, tm), lambda i: (0, 0, i)), both_cols, cols2, cols2, rows, rows, rows]
        + [fixed((width, units))] * 4 + [fixed((4, units))] + [fixed((units, width))] * 4
        + [fixed((1, width))] * 3 + [fixed((experts * head, width))],
        out_specs=[rows, rows, both_rows, both_rows, both_cols, spec((16, tm), lambda i: (0, i))]
        + [fixed((tail, units))] * 4 + [fixed((experts * head, width))],
        out_shape=[shape((tokens, width), BF), shape((tokens, width), F32), shape((2, tokens, LANES), BF),
                   shape((2, tokens, LANES), BF), shape((2, head, tokens), BF), shape((16, tokens), BF)]
        + [shape((tail, units), BF)] * 4 + [shape((experts * head, width), BF)],
        scratch_shapes=[
            pltpu.VMEM((width, 4 * units), F32), pltpu.VMEM((width, 4 * units), F32),
            pltpu.VMEM((experts * head, width), F32), pltpu.VMEM((8, 4 * units), F32),
            pltpu.VMEM((8, width), F32), pltpu.VMEM((16, width), F32),
        ],
        compiler_params=PARAMS,
    )(att, queries, routes_t, gates, x, up, normed, *wes, ebs, *wrs, reduce_bias[None].astype(F32),
      gain2, bias2, wo)
    *ffn_grads, wo_grad = grads

    near, far = group_sum(ffn_grads)
    own = summed(near, far).reshape(dp, tail // dp, units)
    arrived = lax.all_to_all(own, "dp", split_axis=0, concat_axis=0, tiled=True)
    piece = jnp.sum(arrived.astype(F32), axis=0).astype(BF)
    total = sent_to_all(piece, "dp").reshape(tail, units).astype(F32)

    def to_holders(grad):
        each = grad.reshape(experts, 4, head // 4, dp // experts, -1).transpose(0, 3, 1, 2, 4)
        each = each.reshape(dp * 4, head // 4, -1)
        got = lax.all_to_all(each, ("dp", "mp"), split_axis=0, concat_axis=0, tiled=True)
        return jnp.sum(got.astype(F32), axis=0)

    wo_total = to_holders(wo_grad)

    tq = 512
    key_grads = {}
    q_grad = jnp.zeros((2, tokens, LANES), F32)
    per = tokens // tq
    q_block = spec((1, tq, LANES), lambda i: (i // per, i % per, 0))
    t_block = spec((1, head, tq), lambda i: (i // per, 0, i % per))
    for o in (3, 2, 1, 0):
        q_grad, key_grads[o] = pl.pallas_call(
            functools.partial(attend_back_kernel, head=head, tile=tokens),
            grid=(2 * per,),
            in_specs=[SMEM, q_block, q_block, t_block, t_block, fixed((tokens, 2 * head)), q_block],
            out_specs=[q_block, fixed((2 * head, tokens))],
            out_shape=[shape((2, tokens, LANES), F32), shape((2 * head, tokens), BF)],
            input_output_aliases={6: 0},
            scratch_shapes=[
                pltpu.VMEM((tokens, LANES), BF), pltpu.VMEM((tokens, LANES), BF),
                pltpu.VMEM((head, tokens), F32), pltpu.VMEM((head, tokens), F32),
            ],
            compiler_params=PARAMS,
        )(live[o][None], q_rows, do_rows, queries, do_t, pair[o], q_grad)

    far = summed(key_grads[2], swapped(key_grads[3], 1))
    across = swapped(far, 2)
    beside = swapped(key_grads[1], 1)

    tl = 512
    rows = spec((tl, width), lambda i: (i, 0))
    cols2 = spec((2, tl), lambda i: (0, i))
    pair_cols = spec((2 * head, tl), lambda i: (0, i))
    share = experts * head // 4
    input_grad, *last = pl.pallas_call(
        functools.partial(last_kernel, head=head, experts=experts, scale=0.125),
        grid=(tokens // tl,),
        in_specs=[SMEM, spec((2, tl, LANES), lambda i: (0, i, 0)), pair_cols, pair_cols, pair_cols,
                  spec((16, tl), lambda i: (0, i)), cols2, rows, rows, rows, fixed((1, width)),
                  fixed((experts * head, width)), fixed((2 * head, width)), fixed((2 * experts, width))],
        out_specs=[rows] + [fixed((share, width))] * 4 + [fixed((2 * head + 16, width // 4))] * 4,
        out_shape=[shape((tokens, width), F32)] + [shape((share, width), BF)] * 4
        + [shape((2 * head + 16, width // 4), BF)] * 4,
        scratch_shapes=[
            pltpu.VMEM((experts * head, width), F32), pltpu.VMEM((2 * head, width), F32),
            pltpu.VMEM((8, width), F32),
        ],
        compiler_params=PARAMS,
    )(owners, q_grad, key_grads[0], beside, across, logit, routes_t, normed, x, mid_grad, gain1, wq,
      shared_proj.T, router_t)

    near, far = group_sum(last[:4])
    mine = summed(near, far).reshape(experts, head // 4, dp // experts, -1).transpose(0, 2, 1, 3)
    mine = mine.reshape(dp, head // 4, -1)
    got = lax.all_to_all(mine, "dp", split_axis=0, concat_axis=0, tiled=True)
    wq_total = jnp.sum(got.astype(F32), axis=0)
    near, far = group_sum(last[4:])
    ends = jnp.sum(sent_to_all(summed(near, far), "dp").astype(F32), axis=0)

    block = width // 4
    cut = lax.dynamic_slice_in_dim(total[2 * width : 2 * width + 16], me * block, block, axis=1)
    return (
        block_out.reshape(1, tokens, width),
        input_grad.reshape(1, tokens, width),
        ends[2 * head],
        ends[2 * head + 1],
        cut[8 : 8 + experts].T,
        ends[: 2 * head].T,
        wq_total,
        wo_total,
        cut[1],
        cut[2],
        total[:width],
        total[2 * width + 3],
        total[width : 2 * width].T,
        cut[0],
    )


def solution(mesh):
    both = P("dp", "mp", None)
    table = P("mp", "dp")
    placed = (
        both, both, P("dp"), P(), P(), P(), P(), table, table, P(), P(), P(None, "mp"), P("mp"),
        P("mp", None), P(), both,
    )
    given = (
        both, both, P("mp"), P("mp"), P("mp", None), P("mp", None), table, table, P("mp"), P("mp"),
        P(None, "mp"), P("mp"), P("mp", None), P("mp"),
    )
    return jax.shard_map(on_device, mesh=mesh, in_specs=placed, out_specs=given, check_vma=False)
```

time: 1470 us -> 381 us (0.26)
  matrix products: 564 us -> 0 us
  local copies, waits for them, and re-layouts: 364 us -> 17.4 us
  other arithmetic: 248 us -> 10.3 us
  Pallas kernels: 0 us -> 205 us
  blocking collectives: 186 us -> 0 us
  starting transfers between devices: 6.49 us -> 45.3 us
  waiting for transfers between devices: 68.1 us -> 99.7 us
  between operations: 17.1 us -> 1.63 us
    dot_general x77 -> x0, matrix products: 564 us -> none  [the longest x16 149 us: scores_of(): jnp.einsum('qh,kh->qk', query_block, keys, preferred_element_type=jnp.flo...]
    pallas_call x0 -> x9, Pallas kernels: none -> 205 us  [the longest x4 97 us: on_device(): pl.pallas_call(functools.partial(attend_back_kernel, head=head, tile=toke...]
    gather x10 -> x0, local copies, waits for them, and re-layouts: 196 us -> none  [the longest x1 36.7 us: on_device(): branch_grad_slots = branch_grad[slot_source] * slot_live[:, None]]
    reduce_sum x18 -> x4, other arithmetic: 105 us -> 1.54 us  [the longest x1 0.7 us: to_holders(): return jnp.sum(got.astype(F32), axis=0)]
    convert_element_type x23 -> x10, other arithmetic: 106 us -> 7.77 us  [the longest x7 6.19 us: summed(): return (a.astype(F32) + b.astype(F32)).astype(BF)]
    psum x1 -> x0, blocking collectives: 95.8 us -> none  [on_device(): lax.psum((shares[2], shares[3], shares[4], shares[5], shares[6], shares[7...]
    all_gather x5 -> x0, blocking collectives: 84.6 us -> none  [the longest x1 33.7 us: on_device(): lax.all_gather(output_rows, 'dp', axis=1, tiled=True)]
    all_to_all x1 -> x7, waiting for transfers between devices: 0.01 us -> 68.2 us  [the longest x4 42.4 us: sent_to_all(): return lax.all_to_all(wide, axes, split_axis=0, concat_axis=0, tiled=True)]
  transfers between devices with their start and end apart: 11 -> 31, of which waited for: 3 -> 11; matrix products, arithmetic and copies ran while one was open for 41% -> 4% of each run, Pallas kernels for 0% -> 40%
where the time goes in v1:
time: 381 us; the launch traced here: 380 us
  Pallas kernels  205 us (54%)
  waiting for transfers between devices  99.7 us (26%)
  starting transfers between devices  45.3 us (12%)
  local copies, waits for them, and re-layouts  17.4 us (5%)
  other arithmetic  10.3 us (3%)
    pallas_call x4, Pallas kernels, on_device(): pl.pallas_call(functools.partial(attend_back_kernel, head=head, tile=toke...  97 us
    pallas_call x1, Pallas kernels, on_device(): pl.pallas_call(functools.partial(middle_kernel, head=head, experts=expert...  54.3 us
    all_to_all x4, waiting for transfers between devices, sent_to_all(): return lax.all_to_all(wide, axes, split_axis=0, concat_axis=0, tiled=True)  42.4 us
    pallas_call x1, Pallas kernels, on_device(): pl.pallas_call(functools.partial(attend_kernel, head=head, span=4 * token...  33 us
    ppermute x24, waiting for transfers between devices, swapped(): return lax.ppermute(value, 'mp', [(i, i ^ bit) for i in range(4)])  31.5 us
    all_to_all x1, waiting for transfers between devices, on_device(): arrived = lax.all_to_all(own, 'dp', split_axis=0, concat_axis=0, tiled=True)  21.7 us
    all_to_all x4, starting transfers between devices, sent_to_all(): return lax.all_to_all(wide, axes, split_axis=0, concat_axis=0, tiled=True)  17.4 us
    ppermute x24, starting transfers between devices, swapped(): return lax.ppermute(value, 'mp', [(i, i ^ bit) for i in range(4)])  15 us
  transfers between devices with their start and end apart: 31, of which 11 were waited for; matrix products, arithmetic and copies ran while one was open for 4% of the time, Pallas kernels for 40%

profile of v1, /device:TPU:0, one launch (start us, length us, event | category | flops | bytes accessed | tf_op | source)
XLA Modules:
  0.0 379.7 jit_solution(8644433822979223272)
XLA Ops:
  2.2 7.3 %all-to-all-start = ((bf16[32,16,512]{2,1,0:T(8,128)(2,1)}), bf16[32,16,512]{2,1,0:T(8,128)(2,1)S(1)}, u32[]{:S(2)}, u32[]{:S(2)}) async-start(bf16[32,16,512]{2,1,0:T(8,128)(2,1)} %broadcast_in_dim.22), calls=%async_computation | async-start | bytes 1048576 | tf_op jit(solution)/shard_map/all_to_all | solution.py:359
  10.8 5.2 %shard_map.263 = (bf16[2048,512]{1,0:T(8,128)(2,1)}, bf16[2048,128]{1,0:T(8,128)(2,1)}, f32[2,2048]{1,0:T(2,128)}) custom-call(bf16[2048,512]{1,0:T(8,128)(2,1)} %bitcast.41, f32[1,512]{1,0:T(1,128)} %bitcast.56, f32[1,512]{1,0:T(1,128)} %bitcast.59, bf16[16,512]{1,0:T(8,128)(2,1)} %concatenate.6.router, bf16[512,128]{1,0:T(8,128)(2,1)} %proj.1, ...), custom_call_target="tpu_custom_call" | custom-call | tf_op jit(solution)/shard_map/pallas_call | solution.py:411
  17.9 7.2 %all-to-all-done = bf16[32,16,512]{2,1,0:T(8,128)(2,1)S(1)} async-done(((bf16[32,16,512]{2,1,0:T(8,128)(2,1)}), bf16[32,16,512]{2,1,0:T(8,128)(2,1)S(1)}, u32[]{:S(2)}, u32[]{:S(2)}) %all-to-all-start) | async-done | bytes 524320 | tf_op jit(solution)/shard_map/all_to_all | solution.py:359
  25.9 4.6 %shard_map.264.q.qt = bf16[2,64,2048]{2,1,0:T(8,128)(2,1)} custom-call(bf16[2048,512]{1,0:T(8,128)(2,1)} %get-tuple-element.50.normed, bf16[512,512]{1,0:T(8,128)(2,1)} %bitcast.44, s32[2,2048]{1,0:T(2,128)} %bitcast.51), custom_call_target="tpu_custom_call" | custom-call | tf_op jit(solution)/shard_map/pallas_call | solution.py:422
  33.4 3.1 all-to-all-start.1
  38.4 22.8 %collective-permute-done.7 = bf16[1,512]{1,0:T(2,128)(2,1)S(1)} collective-permute-done((bf16[1,512]{1,0:T(2,128)(2,1)S(1)}, bf16[1,512]{1,0:T(2,128)(2,1)S(1)}, u32[]{:S(2)}, u32[]{:S(2)}) %collective-permute-start.7) | collective-permute-done | bytes 1056 | tf_op jit(solution)/shard_map/ppermute | solution.py:338
  66.2 33.0 %shard_map.265.att = f32[2,72,2048]{2,1,0:T(8,128)} custom-call(s32[4]{0:T(128)} %subtract_clamp_fusion.live, bf16[2,64,2048]{2,1,0:T(8,128)(2,1)} %shard_map.264.q.qt, bf16[2048,128]{1,0:T(8,128)(2,1)} %get-tuple-element.52.p0.pair, bf16[2048,128]{1,0:T(8,128)(2,1)} %copy-done.2, bf16[2048,128]{1,0:T(8,128)(2,1)} %copy-done.3, bf16[2048,128]{1,0:T(8,128)(2,1)} %copy-done.4), custom_call_target="tpu_custom_call" | custom-call | tf_op jit(solution)/shard_map/pallas_call | solution.py:439
  100.1 54.3 %shard_map.266 = (bf16[2048,512]{1,0:T(8,128)(2,1)}, f32[2048,512]{1,0:T(8,128)}, bf16[2,2048,128]{2,1,0:T(8,128)(2,1)}, bf16[2,2048,128]{2,1,0:T(8,128)(2,1)}, ...) custom-call(f32[2,72,2048]{2,1,0:T(8,128)} %shard_map.265.att, ...), custom_call_target="tpu_custom_call" | custom-call | tf_op jit(solution)/shard_map/pallas_call | solution.py:458
  156.9 24.1 %shard_map.267 = (f32[2,2048,128]{2,1,0:T(8,128)}, bf16[128,2048]{1,0:T(8,128)(2,1)}) custom-call(s32[1]{0:T(128)} %get-tuple-element.135.live, bf16[2,2048,128]{2,1,0:T(8,128)(2,1)} %get-tuple-element.59.q, bf16[2,2048,128]{2,1,0:T(8,128)(2,1)} %get-tuple-element.60.do, bf16[2,64,2048]{2,1,0:T(8,128)(2,1)} %shard_map.264.q.qt, ...), custom_call_target="tpu_custom_call", output_to_operand_aliasing={{0}: (6, {})} | custom-call | tf_op jit(solution)/shard_map/pallas_call | solution.py:500
  181.6 24.4 %shard_map.268 = (f32[2,2048,128]{2,1,0:T(8,128)}, bf16[128,2048]{1,0:T(8,128)(2,1)}) custom-call(s32[1]{0:T(128)} %get-tuple-element.136.live, bf16[2,2048,128]{2,1,0:T(8,128)(2,1)} %get-tuple-element.59.q, bf16[2,2048,128]{2,1,0:T(8,128)(2,1)} %get-tuple-element.60.do, bf16[2,64,2048]{2,1,0:T(8,128)(2,1)} %shard_map.264.q.qt, ...), custom_call_target="tpu_custom_call", output_to_operand_aliasing={{0}: (6, {})} | custom-call | tf_op jit(solution)/shard_map/pallas_call | solution.py:500
  205.9 24.3 %shard_map.269 = (f32[2,2048,128]{2,1,0:T(8,128)}, bf16[128,2048]{1,0:T(8,128)(2,1)}) custom-call(s32[1]{0:T(128)} %get-tuple-element.137.live, bf16[2,2048,128]{2,1,0:T(8,128)(2,1)} %get-tuple-element.59.q, bf16[2,2048,128]{2,1,0:T(8,128)(2,1)} %get-tuple-element.60.do, bf16[2,64,2048]{2,1,0:T(8,128)(2,1)} %shard_map.264.q.qt, ...), custom_call_target="tpu_custom_call", output_to_operand_aliasing={{0}: (6, {})} | custom-call | tf_op jit(solution)/shard_map/pallas_call | solution.py:500
  233.3 3.6 all-to-all-start.6
  238.2 24.2 %shard_map.270 = (f32[2,2048,128]{2,1,0:T(8,128)}, bf16[128,2048]{1,0:T(8,128)(2,1)}) custom-call(s32[1]{0:T(128)} %get-tuple-element.138.live, bf16[2,2048,128]{2,1,0:T(8,128)(2,1)} %get-tuple-element.59.q, bf16[2,2048,128]{2,1,0:T(8,128)(2,1)} %get-tuple-element.60.do, bf16[2,64,2048]{2,1,0:T(8,128)(2,1)} %shard_map.264.q.qt, ...), custom_call_target="tpu_custom_call", output_to_operand_aliasing={{0}: (6, {})} | custom-call | tf_op jit(solution)/shard_map/pallas_call | solution.py:500
  263.4 11.1 %shard_map.271 = (f32[2048,512]{1,0:T(8,128)}, bf16[128,512]{1,0:T(8,128)(2,1)}, bf16[128,512]{1,0:T(8,128)(2,1)}, bf16[128,512]{1,0:T(8,128)(2,1)}, bf16[128,51...) custom-call(s32[4]{0:T(128)} %iota_xor_fusion.where, ...), custom_call_target="tpu_custom_call" | custom-call | tf_op jit(solution)/shard_map/pallas_call | solution.py:523
  278.9 3.9 %collective-permute-done.23 = bf16[128,512]{1,0:T(8,128)(2,1)S(1)} collective-permute-done((bf16[128,512]{1,0:T(8,128)(2,1)S(1)}, bf16[128,512]{1,0:T(8,128)(2,1)S(1)}, u32[]{:S(2)}, u32[]{:S(2)}) %collective-permute-start.23) | collective-permute-done | bytes 131104 | tf_op jit(solution)/shard_map/ppermute | solution.py:338
  284.4 5.7 %all-to-all-start.5 = ((bf16[8,16,512]{2,1,0:T(8,128)(2,1)}), bf16[8,16,512]{2,1,0:T(8,128)(2,1)S(1)}, u32[]{:S(2)}, u32[]{:S(2)}) async-start(bf16[8,16,512]{2,1,0:T(8,128)(2,1)} %bitcast.23), calls=%async_computation.5 | async-start | bytes 262144 | tf_op jit(solution)/shard_map/all_to_all | solution.py:543
  290.2 3.2 add_convert_fusion
  293.3 4.1 %all-to-all-done.5 = bf16[8,16,512]{2,1,0:T(8,128)(2,1)S(1)} async-done(((bf16[8,16,512]{2,1,0:T(8,128)(2,1)}), bf16[8,16,512]{2,1,0:T(8,128)(2,1)S(1)}, u32[]{:S(2)}, u32[]{:S(2)}) %all-to-all-start.5) | async-done | bytes 131104 | tf_op jit(solution)/shard_map/all_to_all | solution.py:543
  297.5 3.6 all-to-all-start.3
  306.4 21.7 %all-to-all-done.3 = bf16[8,144,512]{2,1,0:T(8,128)(2,1)S(1)} async-done(((bf16[8,144,512]{2,1,0:T(8,128)(2,1)}), bf16[8,144,512]{2,1,0:T(8,128)(2,1)S(1)}, u32[]{:S(2)}, u32[]{:S(2)}) %all-to-all-start.3) | async-done | bytes 1179680 | tf_op jit(solution)/shard_map/all_to_all | solution.py:481
  328.8 3.4 all-to-all-start.2
  332.4 9.6 %all-to-all-done.2 = bf16[8,144,128]{2,1,0:T(8,128)(2,1)S(1)} async-done(((bf16[8,144,128]{2,1,0:T(8,128)(2,1)}), bf16[8,144,128]{2,1,0:T(8,128)(2,1)S(1)}, u32[]{:S(2)}, u32[]{:S(2)}) %all-to-all-start.2) | async-done | bytes 294944 | tf_op jit(solution)/shard_map/all_to_all | solution.py:359
  343.2 3.6 all-to-all-start.4
  349.4 25.7 %all-to-all-done.4 = bf16[8,144,512]{2,1,0:T(8,128)(2,1)S(1)} async-done(((bf16[8,144,512]{2,1,0:T(8,128)(2,1)}), bf16[8,144,512]{2,1,0:T(8,128)(2,1)S(1)}, u32[]{:S(2)}, u32[]{:S(2)}) %all-to-all-start.4) | async-done | bytes 1179680 | tf_op jit(solution)/shard_map/all_to_all | solution.py:359
  (123 shorter events, 44.4 us)
Async XLA Ops:
  2.2 22.9 %all-to-all-start = ((bf16[32,16,512]{2,1,0:T(8,128)(2,1)}), bf16[32,16,512]{2,1,0:T(8,128)(2,1)S(1)}, u32[]{:S(2)}, u32[]{:S(2)}) async-start(bf16[32,16,512]{2,1,0:T(8,128)(2,1)} %broadcast_in_dim.22), calls=%async_computation | async-start | bytes 1048576 | tf_op jit(solution)/shard_map/all_to_all | solution.py:359
  16.1 22.3 %collective-permute-start.1 = (bf16[2048,128]{1,0:T(8,128)(2,1)}, bf16[2048,128]{1,0:T(8,128)(2,1)S(1)}, u32[]{:S(2)}, u32[]{:S(2)}) collective-permute-start(bf16[2048,128]{1,0:T(8,128)(2,1)} %get-tuple-element.52.p0.pair), channel_id=1, source_target_pairs={{0,2},{1,3},{2,0},{3,1},{4,6},{5,7},{6,4},{7,5},{8,10},{9,11},{10,... | collective-permute-start | bytes 1572872 | tf_op jit(solution)/shard_map/ppermute | solution.py:338
  17.9 43.3 %collective-permute-start = (bf16[2048,128]{1,0:T(8,128)(2,1)}, bf16[2048,128]{1,0:T(8,128)(2,1)S(1)}, u32[]{:S(2)}, u32[]{:S(2)}) collective-permute-start(bf16[2048,128]{1,0:T(8,128)(2,1)} %get-tuple-element.52.p0.pair), channel_id=1, source_target_pairs={{0,1},{1,0},{2,3},{3,2},{4,5},{5,4},{6,7},{7,6},{8,9},{9,8},{10,11... | collective-permute-start | bytes 1572872 | tf_op jit(solution)/shard_map/ppermute | solution.py:338
  30.5 31.9 %collective-permute-start.10 = (bf16[512,512]{1,0:T(8,128)(2,1)S(1)}, bf16[512,512]{1,0:T(8,128)(2,1)}, u32[]{:S(2)}, u32[]{:S(2)}) collective-permute-start(bf16[512,512]{1,0:T(8,128)(2,1)S(1)} %copy-done.8), channel_id=1, source_target_pairs={{0,2},{1,3},{2,0},{3,1},{4,6},{5,7},{6,4},{7,5},{8,10},{9,11},{10,... | collective-permute-start | bytes 1572872 | tf_op jit(solution)/shard_map/ppermute | solution.py:338
  31.5 31.3 %collective-permute-start.4 = (bf16[512,512]{1,0:T(8,128)(2,1)S(1)}, bf16[512,512]{1,0:T(8,128)(2,1)}, u32[]{:S(2)}, u32[]{:S(2)}) collective-permute-start(bf16[512,512]{1,0:T(8,128)(2,1)S(1)} %copy-done.7), channel_id=1, source_target_pairs={{0,2},{1,3},{2,0},{3,1},{4,6},{5,7},{6,4},{7,5},{8,10},{9,11},{10,... | collective-permute-start | bytes 1572872 | tf_op jit(solution)/shard_map/ppermute | solution.py:338
  33.4 65.8 %all-to-all-start.1 = ((bf16[32,16,512]{2,1,0:T(8,128)(2,1)}), bf16[32,16,512]{2,1,0:T(8,128)(2,1)S(1)}, u32[]{:S(2)}, u32[]{:S(2)}) async-start(bf16[32,16,512]{2,1,0:T(8,128)(2,1)} %broadcast_in_dim.50), calls=%async_computation.1 | async-start | bytes 1048576 | tf_op jit(solution)/shard_map/all_to_all | solution.py:359
  36.5 24.6 %collective-permute-start.7 = (bf16[1,512]{1,0:T(2,128)(2,1)S(1)}, bf16[1,512]{1,0:T(2,128)(2,1)S(1)}, u32[]{:S(2)}, u32[]{:S(2)}) collective-permute-start(bf16[1,512]{1,0:T(2,128)(2,1)S(1)} %broadcast_in_dim.23), channel_id=1, source_target_pairs={{0,2},{1,3},{2,0},{3,1},{4,6},{5,7},{6,4},{7,5},{8,10},{9,11},{10,... | collective-permute-start | bytes 3080 | tf_op jit(solution)/shard_map/ppermute | solution.py:338
  38.4 23.3 %collective-permute-start.6 = (bf16[1,512]{1,0:T(2,128)(2,1)S(1)}, bf16[1,512]{1,0:T(2,128)(2,1)S(1)}, u32[]{:S(2)}, u32[]{:S(2)}) collective-permute-start(bf16[1,512]{1,0:T(2,128)(2,1)S(1)} %broadcast_in_dim.23), channel_id=1, source_target_pairs={{0,1},{1,0},{2,3},{3,2},{4,5},{5,4},{6,7},{7,6},{8,9},{9,8},{10,11... | collective-permute-start | bytes 3080 | tf_op jit(solution)/shard_map/ppermute | solution.py:338
  61.7 37.6 %collective-permute-start.3 = (bf16[512,512]{1,0:T(8,128)(2,1)S(1)}, bf16[512,512]{1,0:T(8,128)(2,1)}, u32[]{:S(2)}, u32[]{:S(2)}) collective-permute-start(bf16[512,512]{1,0:T(8,128)(2,1)S(1)} %copy-done.7), channel_id=1, source_target_pairs={{0,1},{1,0},{2,3},{3,2},{4,5},{5,4},{6,7},{7,6},{8,9},{9,8},{10,11... | collective-permute-start | bytes 1572872 | tf_op jit(solution)/shard_map/ppermute | solution.py:338
  62.3 36.9 %collective-permute-start.9 = (bf16[512,512]{1,0:T(8,128)(2,1)S(1)}, bf16[512,512]{1,0:T(8,128)(2,1)}, u32[]{:S(2)}, u32[]{:S(2)}) collective-permute-start(bf16[512,512]{1,0:T(8,128)(2,1)S(1)} %copy-done.8), channel_id=1, source_target_pairs={{0,1},{1,0},{2,3},{3,2},{4,5},{5,4},{6,7},{7,6},{8,9},{9,8},{10,11... | collective-permute-start | bytes 1572872 | tf_op jit(solution)/shard_map/ppermute | solution.py:338
  62.5 36.8 %collective-permute-start.11 = (bf16[512,512]{1,0:T(8,128)(2,1)}, bf16[512,512]{1,0:T(8,128)(2,1)}, u32[]{:S(2)}, u32[]{:S(2)}) collective-permute-start(bf16[512,512]{1,0:T(8,128)(2,1)} %collective-permute-done.10.wr2), channel_id=1, source_target_pairs={{0,1},{1,0},{2,3},{3,2},{4,5},{5,4},{6,7},{7,6},{8,9},{9,8},{10,11... | collective-permute-start | bytes 1572872 | tf_op jit(solution)/shard_map/ppermute | solution.py:338
  62.8 36.4 %collective-permute-start.5 = (bf16[512,512]{1,0:T(8,128)(2,1)}, bf16[512,512]{1,0:T(8,128)(2,1)}, u32[]{:S(2)}, u32[]{:S(2)}) collective-permute-start(bf16[512,512]{1,0:T(8,128)(2,1)} %collective-permute-done.4.we2), channel_id=1, source_target_pairs={{0,1},{1,0},{2,3},{3,2},{4,5},{5,4},{6,7},{7,6},{8,9},{9,8},{10,11... | collective-permute-start | bytes 1572872 | tf_op jit(solution)/shard_map/ppermute | solution.py:338
  154.4 77.7 %collective-permute-start.19 = (bf16[1152,512]{1,0:T(8,128)(2,1)}, bf16[1152,512]{1,0:T(8,128)(2,1)S(1)}, u32[]{:S(2)}, u32[]{:S(2)}) collective-permute-start(bf16[1152,512]{1,0:T(8,128)(2,1)} %get-tuple-element.80), channel_id=1, source_target_pairs={{0,1},{1,0},{2,3},{3,2},{4,5},{5,4},{6,7},{7,6},{8,9},{9,8},{10,11... | collective-permute-start | bytes 3538952 | tf_op jit(solution)/shard_map/ppermute | solution.py:338
  181.0 49.4 %collective-permute-start.13 = (bf16[128,2048]{1,0:T(8,128)(2,1)}, bf16[128,2048]{1,0:T(8,128)(2,1)S(1)}, u32[]{:S(2)}, u32[]{:S(2)}) collective-permute-start(bf16[128,2048]{1,0:T(8,128)(2,1)} %get-tuple-element.69), channel_id=1, source_target_pairs={{0,1},{1,0},{2,3},{3,2},{4,5},{5,4},{6,7},{7,6},{8,9},{9,8},{10,11... | collective-permute-start | bytes 1572872 | tf_op jit(solution)/shard_map/ppermute | solution.py:338
  181.2 108.9 %collective-permute-start.18 = (bf16[1152,512]{1,0:T(8,128)(2,1)}, bf16[1152,512]{1,0:T(8,128)(2,1)}, u32[]{:S(2)}, u32[]{:S(2)}) collective-permute-start(bf16[1152,512]{1,0:T(8,128)(2,1)} %get-tuple-element.78), channel_id=1, source_target_pairs={{0,1},{1,0},{2,3},{3,2},{4,5},{5,4},{6,7},{7,6},{8,9},{9,8},{10,11... | collective-permute-start | bytes 3538952 | tf_op jit(solution)/shard_map/ppermute | solution.py:338
  230.2 32.2 %collective-permute-start.12 = (bf16[128,2048]{1,0:T(8,128)(2,1)}, bf16[128,2048]{1,0:T(8,128)(2,1)S(1)}, u32[]{:S(2)}, u32[]{:S(2)}) collective-permute-start(bf16[128,2048]{1,0:T(8,128)(2,1)} %get-tuple-element.67), channel_id=1, source_target_pairs={{0,1},{1,0},{2,3},{3,2},{4,5},{5,4},{6,7},{7,6},{8,9},{9,8},{10,11... | collective-permute-start | bytes 1572872 | tf_op jit(solution)/shard_map/ppermute | solution.py:338
  230.6 31.8 %collective-permute-start.14 = (bf16[128,2048]{1,0:T(8,128)(2,1)S(1)}, bf16[128,2048]{1,0:T(8,128)(2,1)S(1)}, u32[]{:S(2)}, u32[]{:S(2)}) collective-permute-start(bf16[128,2048]{1,0:T(8,128)(2,1)S(1)} %add_convert_fusion.3), channel_id=1, source_target_pairs={{0,2},{1,3},{2,0},{3,1},{4,6},{5,7},{6,4},{7,5},{8,10},{9,11},{10,... | collective-permute-start | bytes 1572872 | tf_op jit(solution)/shard_map/ppermute | solution.py:338
  232.4 57.7 %collective-permute-start.20 = (bf16[1152,512]{1,0:T(8,128)(2,1)S(1)}, bf16[1152,512]{1,0:T(8,128)(2,1)}, u32[]{:S(2)}, u32[]{:S(2)}) collective-permute-start(bf16[1152,512]{1,0:T(8,128)(2,1)S(1)} %add_convert_fusion.1), channel_id=1, source_target_pairs={{0,2},{1,3},{2,0},{3,1},{4,6},{5,7},{6,4},{7,5},{8,10},{9,11},{10,... | collective-permute-start | bytes 3538952 | tf_op jit(solution)/shard_map/ppermute | solution.py:338
  233.3 51.1 %all-to-all-start.6 = ((bf16[32,16,512]{2,1,0:T(8,128)(2,1)}), bf16[32,16,512]{2,1,0:T(8,128)(2,1)S(1)}, u32[]{:S(2)}, u32[]{:S(2)}) async-start(bf16[32,16,512]{2,1,0:T(8,128)(2,1)} %bitcast.49), calls=%async_computation.6 | async-start | bytes 1048576 | tf_op jit(solution)/shard_map/all_to_all | solution.py:488
  277.1 5.7 %collective-permute-start.23 = (bf16[128,512]{1,0:T(8,128)(2,1)S(1)}, bf16[128,512]{1,0:T(8,128)(2,1)S(1)}, u32[]{:S(2)}, u32[]{:S(2)}) collective-permute-start(bf16[128,512]{1,0:T(8,128)(2,1)S(1)} %add_convert_fusion.5), channel_id=1, source_target_pairs={{0,2},{1,3},{2,0},{3,1},{4,6},{5,7},{6,4},{7,5},{8,10},{9,11},{10,... | collective-permute-start | bytes 393224 | tf_op jit(solution)/shard_map/ppermute | solution.py:338
  284.4 13.1 %all-to-all-start.5 = ((bf16[8,16,512]{2,1,0:T(8,128)(2,1)}), bf16[8,16,512]{2,1,0:T(8,128)(2,1)S(1)}, u32[]{:S(2)}, u32[]{:S(2)}) async-start(bf16[8,16,512]{2,1,0:T(8,128)(2,1)} %bitcast.23), calls=%async_computation.5 | async-start | bytes 262144 | tf_op jit(solution)/shard_map/all_to_all | solution.py:543
  297.5 30.6 %all-to-all-start.3 = ((bf16[8,144,512]{2,1,0:T(8,128)(2,1)}), bf16[8,144,512]{2,1,0:T(8,128)(2,1)S(1)}, u32[]{:S(2)}, u32[]{:S(2)}) async-start(bf16[8,144,512]{2,1,0:T(8,128)(2,1)} %bitcast.19), calls=%async_computation.3 | async-start | bytes 2359296 | tf_op jit(solution)/shard_map/all_to_all | solution.py:481
  328.8 13.2 %all-to-all-start.2 = ((bf16[8,144,128]{2,1,0:T(8,128)(2,1)}), bf16[8,144,128]{2,1,0:T(8,128)(2,1)S(1)}, u32[]{:S(2)}, u32[]{:S(2)}) async-start(bf16[8,144,128]{2,1,0:T(8,128)(2,1)} %broadcast_in_dim.52), calls=%async_computation.2 | async-start | bytes 589824 | tf_op jit(solution)/shard_map/all_to_all | solution.py:359
  343.2 31.9 %all-to-all-start.4 = ((bf16[8,144,512]{2,1,0:T(8,128)(2,1)}), bf16[8,144,512]{2,1,0:T(8,128)(2,1)S(1)}, u32[]{:S(2)}, u32[]{:S(2)}) async-start(bf16[8,144,512]{2,1,0:T(8,128)(2,1)} %broadcast_in_dim.53), calls=%async_computation.4 | async-start | bytes 2359296 | tf_op jit(solution)/shard_map/all_to_all | solution.py:359
  (28 other events, 299.9 us)
